TPU v7x, 32 devices: a whole 2x2x4 slice. The times are simulated.
32 devices in a mesh: groups: 2 (over y), seq: 16 (over z, x, core).
Axes of the slice: x: 2, y: 2, z: 4, core: 2. Of those that a mesh axis runs over, the one named last changes fastest.
Arguments:
- tokens: bfloat16 [16384, 768], P(('groups', 'seq')), parts along dimension 0, may hold values from -6 to 6
- weight: bfloat16 [768, 3, 768], P('seq'), may hold values from -0.125 to 0.125
- cotangent: bfloat16 [16384, 768], P(('groups', 'seq')), parts along dimension 0, may hold values from -6 to 6
Outputs:
- output: bfloat16 [16384, 768], P(('groups', 'seq')), parts along dimension 0
- d_tokens: bfloat16 [16384, 768], P(('groups', 'seq')), parts along dimension 0
- d_weight: float32 [1536, 3, 768], P(('groups', 'seq')), parts along dimension 0
There are 2 independent parts, one for each index of `groups`. A program takes and returns all parts, laid end to end along the dimension named above; an argument that names none is the same for every part. Nothing has to cross between parts.
All inputs are finite; a program needn't handle non-finite values.
Results may differ from a plain program's by a relative error of at most 0.0054.
Values may be sent and summed in bfloat16 or wider, within the bound.
A program may use at most 64 MiB of HBM per device.

v0:
```python
import jax
import jax.numpy as jnp
from jax import lax
from jax.sharding import PartitionSpec as P

SPAN = 2


def shifted(value, axis, steps):
    count = lax.axis_size(axis)
    first, last = (max(0, -steps), min(count, count - steps))
    return lax.ppermute(value, axis, [(source, source + steps) for source in range(first, last)])


def from_lower(values):
    return shifted(values, "seq", SPAN)


def received_upper(values):
    return shifted(values, "seq", -SPAN)


def shards(tokens, weight, cotangent):
    rows = tokens.shape[0]
    width = tokens.shape[1]
    seq_count = lax.axis_size("seq")
    x = tokens.astype(jnp.float32)
    inv = lax.rsqrt(jnp.mean(x * x, axis=1, keepdims=True) + 1e-06)
    normalized_rows = (x * inv).astype(jnp.bfloat16)
    filter_taps = jnp.concatenate(
        [from_lower(normalized_rows), normalized_rows, received_upper(normalized_rows)], axis=1
    )
    full_weight = lax.all_gather(weight, "seq", axis=0, tiled=True)
    pre = lax.dot_general(
        filter_taps,
        full_weight.reshape(width, 3 * width),
        (((1,), (1,)), ((), ())),
        preferred_element_type=jnp.float32,
    )
    output = (x + jax.nn.gelu(pre)).astype(jnp.bfloat16)
    slope = jax.jvp(jax.nn.gelu, (pre,), (jnp.ones_like(pre),))[1]
    grad_out = cotangent.astype(jnp.float32)
    preactivation_gradient = (grad_out * slope).astype(jnp.bfloat16)
    normalized_gradient = jnp.dot(
        received_upper(preactivation_gradient),
        full_weight[:, 0, :],
        preferred_element_type=jnp.float32,
    )
    normalized_gradient = normalized_gradient + jnp.dot(
        preactivation_gradient, full_weight[:, 1, :], preferred_element_type=jnp.float32
    )
    normalized_gradient = normalized_gradient + jnp.dot(
        from_lower(preactivation_gradient), full_weight[:, 2, :], preferred_element_type=jnp.float32
    )
    inner = jnp.mean(normalized_gradient * x, axis=1, keepdims=True)
    d_tokens = (grad_out + inv * normalized_gradient - x * inv * inv * inv * inner).astype(
        jnp.bfloat16
    )
    term = lax.dot_general(
        preactivation_gradient,
        filter_taps,
        (((0,), (0,)), ((), ())),
        preferred_element_type=jnp.float32,
    )
    owned = lax.psum_scatter(term, "seq", scatter_dimension=0, tiled=True)
    scale_factor = 1.0 / jnp.sqrt(jnp.float32(rows * seq_count))
    d_weight = (owned * scale_factor).reshape(owned.shape[0], 3, width)
    return (output, d_tokens, d_weight)


def solution(mesh):
    placed = (P(("groups", "seq"), None), P("seq", None, None), P(("groups", "seq"), None))
    return jax.shard_map(
        shards,
        mesh=mesh,
        in_specs=placed,
        out_specs=(
            P(("groups", "seq"), None),
            P(("groups", "seq"), None),
            P(("groups", "seq"), None, None),
        ),
        check_vma=False,
    )
```

profile of v0, /device:TPU:0, one launch (start us, length us, event | category | flops | bytes accessed | tf_op | source)
XLA Modules:
  0.0 201.4 jit_solution(5340178880958267721)
XLA Ops:
  7.2 0.0 all-gather.2.cloned.1.call-start
  7.2 0.7 all-gather.2.cloned.1.call-update
  7.9 0.0 reduce-scatter.2.cloned.1.call-start
  7.9 1.4 fusion.17
  9.3 1.3 fusion.1
  10.7 0.0 copy-start
  10.7 0.0 copy-start.2
  10.7 1.4 collective-permute-start.1
  12.1 6.4 %collective-permute-start = (bf16[512,768]{1,0:T(8,128)(2,1)S(1)}, bf16[512,768]{1,0:T(8,128)(2,1)}, u32[]{:S(2)}, u32[]{:S(2)}) collective-permute-start(bf16[512,768]{1,0:T(8,128)(2,1)S(1)} %fusion.1), channel_id=1, source_target_pairs={{0,2},{1,3},{2,4},{3,5},{4,6},{5,7},{6,8},{7,9},{8,10},{9,11},{10,... | collective-permute-start | bytes 2359304 | tf_op jit(solution)/shard_map/ppermute | solution.py:12
  18.5 57.6 %all-gather.2.cloned.1.call-done = bf16[768,3,768]{2,0,1:T(8,128)(2,1)} async-done(((bf16[48,3,768]{2,0,1:T(8,128)(2,1)}), bf16[768,3,768]{2,0,1:T(8,128)(2,1)}) %all-gather.2.cloned.1.call-update) | async-done | bytes 3538960 | tf_op jit(solution)/shard_map/all_gather | solution.py:33
  76.1 6.1 %copy.9 = bf16[768,3,768]{0,2,1:T(8,128)(2,1)} copy(bf16[768,3,768]{2,0,1:T(8,128)(2,1)} %all-gather.2.cloned.1.call-done) | data formatting | bytes 7077888 | tf_op jit(solution)/shard_map/all_gather | solution.py:33
  82.1 0.0 collective-permute-done.1
  82.1 0.0 copy-start.3
  82.2 0.0 collective-permute-done
  82.2 0.9 copy-done.3
  83.0 0.0 copy-done
  83.0 0.0 copy-done.2
  83.0 0.0 copy-start.4
  83.0 6.3 %fusion.6 = (bf16[512,768]{1,0:T(8,128)(2,1)S(1)}, bf16[512,768]{1,0:T(8,128)(2,1)}) fusion(bf16[512,768]{1,0:T(8,128)(2,1)S(1)} %copy-done.2, bf16[512,768]{1,0:T(8,128)(2,1)S(1)} %copy-done, bf16[768,2304]{0,1:T(8,128)(2,1)} %bitcast.23, bf16[512,768]{1,0:T(8,128)(2,1)} %copy-done.3, bf16[512,768]{1,0:T(8,128)(2,1)S(1)} %fusion.1, ...), kind=kOutput, calls=%fused_computation.15 | convolution fusion | flops 1828061184 | bytes 9043968 | tf_op jit(solution)/shard_map/dot_general | solution.py:34
  89.4 0.0 copy-done.4
  89.4 6.1 %fusion.23 = f32[768,2304]{1,0:T(8,128)} fusion(bf16[512,768]{1,0:T(8,128)(2,1)S(1)} %get-tuple-element.12, bf16[512,768]{1,0:T(8,128)(2,1)S(1)} %copy-done.4, bf16[512,768]{1,0:T(8,128)(2,1)S(1)} %fusion.1, bf16[512,768]{1,0:T(8,128)(2,1)} %collective-permute-done), kind=kOutput, calls=%fused_computation.36 | convolution fusion | flops 1819017216 | bytes 10223616 | tf_op jit(solution)/shard_map/dot_general | solution.py:59
  95.5 0.0 reduce-scatter.2.cloned.1.call-update
  95.5 0.0 copy-start.1
  95.5 1.6 collective-permute-start.2
  97.1 4.6 %collective-permute-start.3 = (bf16[512,768]{1,0:T(8,128)(2,1)S(1)}, bf16[512,768]{1,0:T(8,128)(2,1)S(1)}, u32[]{:S(2)}, u32[]{:S(2)}) collective-permute-start(bf16[512,768]{1,0:T(8,128)(2,1)S(1)} %get-tuple-element.12), channel_id=1, source_target_pairs={{0,2},{1,3},{2,4},{3,5},{4,6},{5,7},{6,8},{7,9},{8,10},{9,11},{10,... | collective-permute-start | bytes 2359304 | tf_op jit(solution)/shard_map/ppermute | solution.py:12
  101.7 2.2 %fusion.21 = f32[512,768]{1,0:T(8,128)S(1)} fusion(bf16[512,768]{1,0:T(8,128)(2,1)S(1)} %get-tuple-element.12, bf16[768,3,768]{2,0,1:T(8,128)(2,1)} %all-gather.2.cloned.1.call-done), kind=kOutput, calls=%fused_computation.33 | convolution fusion | flops 603979776 | bytes 3538944 | tf_op jit(solution)/shard_map/dot_general | solution.py:49
  103.8 13.5 %collective-permute-done.2 = bf16[512,768]{1,0:T(8,128)(2,1)S(1)} collective-permute-done((bf16[512,768]{1,0:T(8,128)(2,1)S(1)}, bf16[512,768]{1,0:T(8,128)(2,1)S(1)}, u32[]{:S(2)}, u32[]{:S(2)}) %collective-permute-start.2) | collective-permute-done | bytes 786464 | tf_op jit(solution)/shard_map/ppermute | solution.py:12
  117.3 0.0 copy-done.1
  117.4 0.8 fusion.22
  118.1 23.5 %collective-permute-done.3 = bf16[512,768]{1,0:T(8,128)(2,1)S(1)} collective-permute-done((bf16[512,768]{1,0:T(8,128)(2,1)S(1)}, bf16[512,768]{1,0:T(8,128)(2,1)S(1)}, u32[]{:S(2)}, u32[]{:S(2)}) %collective-permute-start.3) | collective-permute-done | bytes 786464 | tf_op jit(solution)/shard_map/ppermute | solution.py:12
  141.7 1.0 fusion.19
  142.7 1.5 fusion.5
  144.1 48.6 %reduce-scatter.2.cloned.1.call-done = f32[48,2304]{1,0:T(8,128)} async-done(((f32[768,2304]{1,0:T(8,128)}), f32[48,2304]{1,0:T(8,128)}) %reduce-scatter.2.cloned.1.call-update) | async-done | bytes 442384 | tf_op jit(solution)/shard_map/reduce_scatter | solution.py:65
  192.7 1.1 broadcast_multiply_fusion
  193.8 0.8 copy.13
  (2 shorter events, 0.0 us)
Async XLA Ops:
  7.2 68.9 %all-gather.2.cloned.1.call-start = ((), (), s32[]{:S(2)}) async-start(), calls=%async_computation.1 | async-start | bytes 3760128 | tf_op jit(solution)/shard_map/all_gather | solution.py:33
  7.9 184.8 %reduce-scatter.2.cloned.1.call-start = ((), (), s32[]{:S(2)}) async-start(), calls=%async_computation.2 | async-start | bytes 7520256 | tf_op jit(solution)/shard_map/reduce_scatter | solution.py:65
  10.7 72.4 %copy-start = (bf16[512,768]{1,0:T(8,128)(2,1)S(1)}, bf16[512,768]{1,0:T(8,128)(2,1)}, u32[]{:S(2)}) copy-start(bf16[512,768]{1,0:T(8,128)(2,1)} %param.3) | copy-start | bytes 2359300
  10.7 72.4 %copy-start.2 = (bf16[512,768]{1,0:T(8,128)(2,1)S(1)}, bf16[512,768]{1,0:T(8,128)(2,1)}, u32[]{:S(2)}) copy-start(bf16[512,768]{1,0:T(8,128)(2,1)} %param.5) | copy-start | bytes 2359300
  10.7 71.5 %collective-permute-start.1 = (bf16[512,768]{1,0:T(8,128)(2,1)S(1)}, bf16[512,768]{1,0:T(8,128)(2,1)S(1)}, u32[]{:S(2)}, u32[]{:S(2)}) collective-permute-start(bf16[512,768]{1,0:T(8,128)(2,1)S(1)} %fusion.1), channel_id=1, source_target_pairs={{2,0},{3,1},{4,2},{5,3},{6,4},{7,5},{8,6},{9,7},{10,8},{11,9},{12,... | collective-permute-start | bytes 2359304 | tf_op jit(solution)/shard_map/ppermute | solution.py:12
  12.1 70.0 %collective-permute-start = (bf16[512,768]{1,0:T(8,128)(2,1)S(1)}, bf16[512,768]{1,0:T(8,128)(2,1)}, u32[]{:S(2)}, u32[]{:S(2)}) collective-permute-start(bf16[512,768]{1,0:T(8,128)(2,1)S(1)} %fusion.1), channel_id=1, source_target_pairs={{0,2},{1,3},{2,4},{3,5},{4,6},{5,7},{6,8},{7,9},{8,10},{9,11},{10,... | collective-permute-start | bytes 2359304 | tf_op jit(solution)/shard_map/ppermute | solution.py:12
  82.1 0.9 copy-start.3
  83.0 6.3 %copy-start.4 = (bf16[512,768]{1,0:T(8,128)(2,1)S(1)}, bf16[512,768]{1,0:T(8,128)(2,1)}, u32[]{:S(2)}) copy-start(bf16[512,768]{1,0:T(8,128)(2,1)} %copy-done.3) | copy-start | bytes 2359300
  95.5 21.9 %copy-start.1 = (bf16[768,3,768]{2,0,1:T(8,128)(2,1)S(1)}, bf16[768,3,768]{2,0,1:T(8,128)(2,1)}, u32[]{:S(2)}) copy-start(bf16[768,3,768]{2,0,1:T(8,128)(2,1)} %all-gather.2.cloned.1.call-done) | copy-start | bytes 10616836
  95.5 21.9 %collective-permute-start.2 = (bf16[512,768]{1,0:T(8,128)(2,1)S(1)}, bf16[512,768]{1,0:T(8,128)(2,1)S(1)}, u32[]{:S(2)}, u32[]{:S(2)}) collective-permute-start(bf16[512,768]{1,0:T(8,128)(2,1)S(1)} %get-tuple-element.12), channel_id=1, source_target_pairs={{2,0},{3,1},{4,2},{5,3},{6,4},{7,5},{8,6},{9,7},{10,8},{11,9},{12,... | collective-permute-start | bytes 2359304 | tf_op jit(solution)/shard_map/ppermute | solution.py:12
  97.1 44.6 %collective-permute-start.3 = (bf16[512,768]{1,0:T(8,128)(2,1)S(1)}, bf16[512,768]{1,0:T(8,128)(2,1)S(1)}, u32[]{:S(2)}, u32[]{:S(2)}) collective-permute-start(bf16[512,768]{1,0:T(8,128)(2,1)S(1)} %get-tuple-element.12), channel_id=1, source_target_pairs={{0,2},{1,3},{2,4},{3,5},{4,6},{5,7},{6,8},{7,9},{8,10},{9,11},{10,... | collective-permute-start | bytes 2359304 | tf_op jit(solution)/shard_map/ppermute | solution.py:12
Sparse Core Ops, SparseCore 0:
  10.3 65.7 all-gather.1
  95.6 97.0 reduce-scatter.1
where the time goes:
time: 202 us; the launch traced here: 201 us
  waiting for transfers between devices  144 us (71%)
  matrix products  16.4 us (8%)
  between operations  14.1 us (7%)
  starting transfers between devices  14 us (7%)
  local copies, waits for them, and re-layouts  7.74 us (4%)
  other arithmetic  5.21 us (3%)
    all_gather x1, waiting for transfers between devices, shards(): full_weight = lax.all_gather(weight, 'seq', axis=0, tiled=True)  57.6 us
    reduce_scatter x1, waiting for transfers between devices, shards(): owned = lax.psum_scatter(term, 'seq', scatter_dimension=0, tiled=True)  48.6 us
    ppermute x4, waiting for transfers between devices, shifted(): lax.ppermute(value, axis, [(source, source + steps) for source in range(f...  37 us
    ppermute x4, starting transfers between devices, shifted(): lax.ppermute(value, axis, [(source, source + steps) for source in range(f...  13.9 us
    dot_general x1, matrix products, shards(): lax.dot_general(filter_taps, full_weight.reshape(width, 3 * width), (((1,...  6.32 us
    dot_general x1, matrix products, shards(): lax.dot_general(preactivation_gradient, filter_taps, (((0,), (0,)), ((),...  6.1 us
    all_gather x1, local copies, waits for them, and re-layouts, shards(): full_weight = lax.all_gather(weight, 'seq', axis=0, tiled=True)  6.05 us
  transfers between devices with their start and end apart: 6, of which 4 were waited for; matrix products, arithmetic and copies ran while one was open for 7% of the time, Pallas kernels for 0%

commit v1 on v0

--- a/solution.py
+++ b/solution.py
@@ -1,9 +1,358 @@
+import functools
+import math
+
 import jax
 import jax.numpy as jnp
 from jax import lax
+from jax.experimental import pallas as pl
+from jax.experimental.pallas import tpu as pltpu
 from jax.sharding import PartitionSpec as P
 
 SPAN = 2
+MESH = pl.DeviceIdType.MESH
+F32 = jnp.float32
+BF16 = jnp.bfloat16
+
+T_TOK, T_COT, T_UP, T_DOWN, T_SIDE, T_Z, T_Y, T_CORE = 0, 1, 2, 3, 4, 5, 8, 11
+T_OUT, T_DTOK, T_PUP, T_PDOWN, T_RC, T_RX, T_RZ, T_COUNT = 19, 20, 21, 24, 27, 30, 33, 42
+
+
+def kernel(
+    scale, tok_ref, w_ref, cot_ref, out_ref, dtok_ref, dw_ref,
+    xs, gs, taps, grads, weights, gt, gtp, sums, core_send, core_recv,
+    x_send, x_recv, z_sum, z_send, z_recv, outs, dtoks, send_sem, recv_sem,
+):
+    rows, width = tok_ref.shape
+    half = rows // 2
+    shard = w_ref.shape[0]
+    y = lax.axis_index("groups")
+    s = lax.axis_index("seq")
+    z, x, c = s // 4, (s // 2) % 2, s % 2
+    px = (y, s + 2 - 4 * x)
+    pc = (y, s + 1 - 2 * c)
+    py = (1 - y, s)
+    pz = {j: (y, ((z + j) % 4) * 4 + 2 * x + c) for j in (1, 2, 3)}
+    up = pz[1]
+    down = pz[3]
+
+    barrier = pltpu.get_barrier_semaphore()
+    for peer in (px, pc, py, pz[1], pz[2], pz[3]):
+        pl.semaphore_signal(barrier, inc=1, device_id=peer, device_id_type=MESH)
+    pl.semaphore_wait(barrier, 6)
+
+    def remote(t, src, dst, peer):
+        return pltpu.make_async_remote_copy(
+            src_ref=src, dst_ref=dst, send_sem=send_sem.at[t], recv_sem=recv_sem.at[t],
+            device_id=peer, device_id_type=MESH,
+        )
+
+    def block(ref, index, size):
+        return ref.at[pl.ds(pl.multiple_of(index * size, size), size)]
+
+    def w_copy(t, index, peer):
+        place = block(weights, index, shard)
+        return remote(t, place, place, peer)
+
+    tok_copy = remote(T_TOK, block(tok_ref, 1 - x, half), xs.at[x], px)
+    cot_copy = remote(T_COT, block(cot_ref, 1 - x, half), gs.at[x], px)
+    weights[pl.ds(pl.multiple_of(s * shard, shard), shard), :] = w_ref[...]
+    other_x = s + 2 - 4 * x
+    carried = z * 4 + 2 * y + c
+
+    def start_z():
+        for j in (1, 2, 3):
+            w_copy(T_Z + j - 1, carried, pz[j]).start()
+
+    @pl.when(x == y)
+    def _():
+        w_copy(T_SIDE, s, px).start()
+        start_z()
+
+    tok_copy.start()
+    w_copy(T_CORE, s, pc).start()
+
+    up_copy = remote(T_UP, taps.at[pl.ds(2 * half, half)], taps.at[pl.ds(0, half)], up)
+    down_copy = remote(T_DOWN, taps.at[pl.ds(half, half)], taps.at[pl.ds(3 * half, half)], down)
+
+    def normalize(slot):
+        value = xs[slot].astype(F32)
+        inv = lax.rsqrt(jnp.mean(value * value, axis=1, keepdims=True) + 1e-06)
+        start = pl.multiple_of((slot + 1) * half, half)
+        taps[pl.ds(start, half), :] = (value * inv).astype(BF16)
+
+        @pl.when((slot == 0) & (z > 0))
+        def _():
+            down_copy.start()
+
+        @pl.when((slot == 1) & (z < 3))
+        def _():
+            up_copy.start()
+
+    xs[x] = tok_ref[pl.ds(pl.multiple_of(x * half, half), half), :]
+    gs[x] = cot_ref[pl.ds(pl.multiple_of(x * half, half), half), :]
+    normalize(x)
+
+    @pl.when(x != y)
+    def _():
+        w_copy(T_SIDE, other_x, px).wait_recv()
+        start_z()
+        w_copy(T_SIDE, other_x, py).start()
+
+    tok_copy.wait_recv()
+    normalize(1 - x)
+    cot_copy.start()
+
+    @pl.when(z == 0)
+    def _():
+        taps[0:half, :] = jnp.zeros((half, width), BF16)
+        grads[0:half, :] = jnp.zeros((half, width), BF16)
+
+    @pl.when(z == 3)
+    def _():
+        taps[3 * half :, :] = jnp.zeros((half, width), BF16)
+        grads[3 * half :, :] = jnp.zeros((half, width), BF16)
+
+    @pl.when(x == y)
+    def _():
+        w_copy(T_SIDE, other_x, py).wait_recv()
+
+    w_copy(T_CORE + 1, other_x, pc).start()
+    for j in (1, 3, 2):
+        index = ((z + 4 - j) % 4) * 4 + 2 * y + c
+        w_copy(T_Z + j - 1, index, pz[j]).wait_recv()
+        w_copy(T_Y + j - 1, index, py).start()
+        w_copy(T_CORE + 1 + j, index, pc).start()
+    for j in (1, 3, 2):
+        index = ((z + 4 - j) % 4) * 4 + 2 * (1 - y) + c
+        w_copy(T_Y + j - 1, index, py).wait_recv()
+        w_copy(T_CORE + 4 + j, index, pc).start()
+    across = 1 - c
+    own_core = [z * 4 + 2 * x, z * 4 + 2 * (1 - x)]
+    own_core += [((z + 4 - j) % 4) * 4 + 2 * y for j in (1, 2, 3)]
+    own_core += [((z + 4 - j) % 4) * 4 + 2 * (1 - y) for j in (1, 2, 3)]
+    for q, index in enumerate(own_core):
+        w_copy(T_CORE + q, index + across, pc).wait_recv()
+
+    @pl.when(z > 0)
+    def _():
+        up_copy.wait_recv()
+
+    @pl.when(z < 3)
+    def _():
+        down_copy.wait_recv()
+
+    cot_copy.wait_recv()
+
+    part = width // 3
+    root = math.sqrt(2.0 / math.pi)
+
+    def pup(n):
+        cols = pl.ds(pl.multiple_of(n * part, part), part)
+        return remote(
+            T_PUP + n, grads.at[pl.ds(2 * half, half), cols], grads.at[pl.ds(0, half), cols], up
+        )
+
+    def pdown(n):
+        cols = pl.ds(pl.multiple_of(n * part, part), part)
+        return remote(
+            T_PDOWN + n, grads.at[pl.ds(half, half), cols], grads.at[pl.ds(3 * half, half), cols], down
+        )
+
+    @pl.loop(0, 3)
+    def _(n):
+        cols = pl.ds(pl.multiple_of(n * part, part), part)
+        pre = jnp.zeros((rows, part), F32)
+        for k in range(3):
+            pre = pre + lax.dot_general(
+                taps[k * half : k * half + rows, :],
+                weights[cols, k * width : (k + 1) * width],
+                (((1,), (1,)), ((), ())),
+                preferred_element_type=F32,
+            )
+        square = pre * pre
+        bend = jnp.tanh(root * pre * (1.0 + 0.044715 * square))
+        cdf = 0.5 * (1.0 + bend)
+        slope = cdf + 0.5 * pre * (1.0 - bend * bend) * (root * (1.0 + 3 * 0.044715 * square))
+        value = xs[:, :, cols].reshape(rows, part).astype(F32)
+        grad = gs[:, :, cols].reshape(rows, part).astype(F32)
+        outs[:, :, cols] = (value + pre * cdf).astype(BF16).reshape(2, half, part)
+        d_pre = grad * slope
+        grads[half : 3 * half, cols] = d_pre.astype(BF16)
+
+        @pl.when(z < 3)
+        def _():
+            pup(n).start()
+
+        @pl.when(z > 0)
+        def _():
+            pdown(n).start()
+
+        gt[cols, :] = d_pre.T.astype(BF16)
+
+    out_copy = remote(T_OUT, outs.at[1 - x], block(out_ref, x, half), px)
+    out_copy.start()
+    for source in range(16):
+        place = (source % 2) * 8 + ((source // 2) % 2) * 4 + source // 4
+        gtp[place * shard : (place + 1) * shard, :] = gt[source * shard : (source + 1) * shard, :]
+    out_ref[pl.ds(pl.multiple_of(x * half, half), half), :] = outs[x]
+
+    most = 8 * shard
+
+    def core_copy(k):
+        return remote(T_RC + k, core_send.at[k], core_recv.at[k], pc)
+
+    def x_copy(k):
+        return remote(T_RX + k, x_send.at[k], x_recv.at[k], px)
+
+    def z_copy(k, j):
+        there = block(z_send.at[k], (z + j) % 4, shard)
+        return remote(T_RZ + 3 * k + j - 1, there, z_recv.at[k, j - 1], pz[j])
+
+    def weight_term(k):
+        right = taps[k * half : k * half + rows, :]
+        there = gtp[pl.ds(pl.multiple_of((1 - c) * most, most), most), :]
+        core_send[k] = jnp.dot(there, right, preferred_element_type=F32).astype(BF16)
+        core_copy(k).start()
+        here = gtp[pl.ds(pl.multiple_of(c * most, most), most), :]
+        sums[k] = jnp.dot(here, right, preferred_element_type=F32)
+
+    def over_core(k):
+        core_copy(k).wait_recv()
+        there = pl.ds(pl.multiple_of((1 - x) * 4 * shard, 4 * shard), 4 * shard)
+        x_send[k] = (sums[k, there, :] + core_recv[k, there, :].astype(F32)).astype(BF16)
+        x_copy(k).start()
+
+    def over_x(k):
+        x_copy(k).wait_recv()
+        here = pl.ds(pl.multiple_of(x * 4 * shard, 4 * shard), 4 * shard)
+        total = sums[k, here, :] + core_recv[k, here, :].astype(F32) + x_recv[k].astype(F32)
+        z_sum[k] = total
+        z_send[k] = total.astype(BF16)
+        for j in (1, 2, 3):
+            z_copy(k, j).start()
+
+    def over_z(k):
+        total = z_sum[k, pl.ds(pl.multiple_of(z * shard, shard), shard), :]
+        for j in (1, 2, 3):
+            z_copy(k, j).wait_recv()
+            total = total + z_recv[k, j - 1].astype(F32)
+        dw_ref[:, k * width : (k + 1) * width] = total * scale
+
+    def input_gradient(slot):
+        total = jnp.zeros((half, width), F32)
+        for k in range(3):
+            left = grads[pl.ds(pl.multiple_of((slot + 2 - k) * half, half), half), :]
+            total = total + jnp.dot(
+                left, weights[:, k * width : (k + 1) * width], preferred_element_type=F32
+            )
+        value = xs[slot].astype(F32)
+        inv = lax.rsqrt(jnp.mean(value * value, axis=1, keepdims=True) + 1e-06)
+        inner = jnp.mean(total * value, axis=1, keepdims=True)
+        grad = gs[slot].astype(F32)
+        dtoks[slot] = (grad + inv * total - value * inv * inv * inv * inner).astype(BF16)
+
+    dtok_copy = remote(T_DTOK, dtoks.at[1 - x], block(dtok_ref, x, half), px)
+    weight_term(0)
+    weight_term(1)
+    over_core(0)
+    weight_term(2)
+    over_core(1)
+    over_core(2)
+
+    @pl.when(z > 0)
+    def _():
+        for n in range(3):
+            pup(n).wait_recv()
+
+    @pl.when(z < 3)
+    def _():
+        for n in range(3):
+            pdown(n).wait_recv()
+
+    input_gradient(1 - x)
+    dtok_copy.start()
+    over_x(0)
+    input_gradient(x)
+    dtok_ref[pl.ds(pl.multiple_of(x * half, half), half), :] = dtoks[x]
+    over_x(1)
+    over_x(2)
+    over_z(0)
+    over_z(1)
+    over_z(2)
+
+    out_copy.wait_recv()
+    dtok_copy.wait_recv()
+
+    for copy in (tok_copy, cot_copy, out_copy, dtok_copy):
+        copy.wait_send()
+
+    @pl.when(z > 0)
+    def _():
+        down_copy.wait_send()
+        for n in range(3):
+            pdown(n).wait_send()
+
+    @pl.when(z < 3)
+    def _():
+        up_copy.wait_send()
+        for n in range(3):
+            pup(n).wait_send()
+
+    for t in [T_SIDE] + [T_Z + j for j in range(3)] + [T_Y + j for j in range(3)]:
+        w_copy(t, s, px).wait_send()
+    for q in range(8):
+        w_copy(T_CORE + q, s, pc).wait_send()
+    for k in range(3):
+        core_copy(k).wait_send()
+        x_copy(k).wait_send()
+        for j in (1, 2, 3):
+            z_copy(k, j).wait_send()
+
+
+def fused(tokens, weight, cotangent):
+    rows, width = tokens.shape
+    shard = weight.shape[0]
+    half = rows // 2
+    scale = 1.0 / math.sqrt(rows * lax.axis_size("seq"))
+    vmem = pl.BlockSpec(memory_space=pltpu.VMEM)
+    output, d_tokens, d_weight = pl.pallas_call(
+        functools.partial(kernel, scale),
+        out_shape=(
+            jax.ShapeDtypeStruct((rows, width), BF16),
+            jax.ShapeDtypeStruct((rows, width), BF16),
+            jax.ShapeDtypeStruct((shard, 3 * width), F32),
+        ),
+        in_specs=[vmem] * 3,
+        out_specs=(vmem, vmem, vmem),
+        scratch_shapes=[
+            pltpu.VMEM((2, half, width), BF16),
+            pltpu.VMEM((2, half, width), BF16),
+            pltpu.VMEM((4 * half, width), BF16),
+            pltpu.VMEM((4 * half, width), BF16),
+            pltpu.VMEM((width, 3 * width), BF16),
+            pltpu.VMEM((width, rows), BF16),
+            pltpu.VMEM((width, rows), BF16),
+            pltpu.VMEM((3, 8 * shard, width), F32),
+            pltpu.VMEM((3, 8 * shard, width), BF16),
+            pltpu.VMEM((3, 8 * shard, width), BF16),
+            pltpu.VMEM((3, 4 * shard, width), BF16),
+            pltpu.VMEM((3, 4 * shard, width), BF16),
+            pltpu.VMEM((3, 4 * shard, width), F32),
+            pltpu.VMEM((3, 4 * shard, width), BF16),
+            pltpu.VMEM((3, 3, shard, width), BF16),
+            pltpu.VMEM((2, half, width), BF16),
+            pltpu.VMEM((2, half, width), BF16),
+            pltpu.SemaphoreType.DMA((T_COUNT,)),
+            pltpu.SemaphoreType.DMA((T_COUNT,)),
+        ],
+        compiler_params=pltpu.CompilerParams(
+            collective_id=0, has_side_effects=True, vmem_limit_bytes=52 * 1024 * 1024
+        ),
+        cost_estimate=pl.CostEstimate(
+            flops=6 * rows * 3 * width * width, bytes_accessed=6 * rows * width * 2, transcendentals=rows * width
+        ),
+    )(tokens, weight.reshape(shard, 3 * width), cotangent)
+    return output, d_tokens, d_weight.reshape(shard, 3, width)
 
 
 def shifted(value, axis, steps):
@@ -20,7 +369,7 @@
     return shifted(values, "seq", -SPAN)
 
 
-def shards(tokens, weight, cotangent):
+def general(tokens, weight, cotangent):
     rows = tokens.shape[0]
     width = tokens.shape[1]
     seq_count = lax.axis_size("seq")
@@ -70,8 +419,9 @@
 
 def solution(mesh):
     placed = (P(("groups", "seq"), None), P("seq", None, None), P(("groups", "seq"), None))
+    small = mesh.shape["groups"] == 2 and mesh.shape["seq"] == 16
     return jax.shard_map(
-        shards,
+        fused if small else general,
         mesh=mesh,
         in_specs=placed,
         out_specs=(

time: 202 us -> 91.6 us (0.45)
  the two profiles are of different devices: /device:TPU:0 before, /device:TPU:11 now
where the time goes in v1:
time: 91.6 us; the launch traced here: 91.4 us
  Pallas kernels  86.7 us (95%)
  local copies, waits for them, and re-layouts  4.04 us (4%)
    pallas_call x1, Pallas kernels, fused(): pl.pallas_call(functools.partial(kernel, scale), out_shape=(jax.ShapeDtyp...  86.7 us
    unnamed x4, local copies, waits for them, and re-layouts  2.29 us

profile of v1, /device:TPU:11, one launch (start us, length us, event | category | flops | bytes accessed | tf_op | source)
XLA Modules:
  0.0 91.4 jit_solution(4891386963122871807)
XLA Ops:
  0.6 1.0 %copy.11 = bf16[3,6,8,768]{3,2,0,1:T(8,128)(2,1)S(1)} copy(bf16[3,6,8,768]{3,2,1,0:T(8,128)(2,1)} %bitcast.9) | data formatting | bytes 442368 | tf_op jit(solution)/shard_map/reshape | solution.py:354
  1.6 86.7 %shard_map.58 = (bf16[512,768]{1,0:T(8,128)(2,1)S(1)}, bf16[512,768]{1,0:T(8,128)(2,1)}, f32[48,2304]{1,0:T(8,128)S(1)}) custom-call(bf16[512,768]{1,0:T(8,128)(2,1)} %tok_ref.1, bf16[48,2304]{1,0:T(8,128)(2,1)S(1)} %bitcast.7, bf16[512,768]{1,0:T(8,128)(2,1)} %cot_ref.1), custom_call_target="tpu_custom_call" | custom-call | flops 5435817984 | bytes 4718592 | tf_op jit(solution)/shard_map/pallas_call | solution.py:318
  88.3 0.8 copy.13
  89.1 0.0 copy-start
  89.1 0.9 copy.16
  90.0 0.5 copy-done
  90.5 0.9 copy.17
Async XLA Ops:
  89.1 1.4 %copy-start = (bf16[512,768]{1,0:T(8,128)(2,1)S(1)}, bf16[512,768]{1,0:T(8,128)(2,1)}, u32[]{:S(2)}) copy-start(bf16[512,768]{1,0:T(8,128)(2,1)} %get-tuple-element.19) | copy-start | bytes 2359300

commit v2 on v1

--- a/solution.py
+++ b/solution.py
@@ -13,8 +13,9 @@
 F32 = jnp.float32
 BF16 = jnp.bfloat16
 
-T_TOK, T_COT, T_UP, T_DOWN, T_SIDE, T_Z, T_Y, T_CORE = 0, 1, 2, 3, 4, 5, 8, 11
-T_OUT, T_DTOK, T_PUP, T_PDOWN, T_RC, T_RX, T_RZ, T_COUNT = 19, 20, 21, 24, 27, 30, 33, 42
+T_TOK, T_COT, T_UP, T_DOWN, T_SIDE, T_CORE = 0, 1, 2, 3, 4, 6
+T_ZUP, T_ZDOWN, T_YUP, T_YDOWN = 14, 20, 26, 32
+T_OUT, T_DTOK, T_PUP, T_PDOWN, T_RC, T_RX, T_RZ, T_COUNT = 38, 40, 41, 43, 45, 48, 51, 60
 
 
 def kernel(
@@ -53,21 +54,59 @@
         place = block(weights, index, shard)
         return remote(t, place, place, peer)
 
+    most_cols = weights.shape[1] // 2
+
+    def half_copy(t, index, side, peer):
+        place = weights.at[
+            pl.ds(pl.multiple_of(index * shard, shard), shard),
+            pl.ds(pl.multiple_of(side * most_cols, most_cols), most_cols),
+        ]
+        return remote(t, place, place, peer)
+
+    def at(d, q):
+        return (z + d) * 4 + (2 * x + c if q == 0 else 2 * (1 - x) + c)
+
+    def send_z(d, q):
+        @pl.when((z < 3) & (z - d >= 0))
+        def _():
+            half_copy(T_ZUP + 2 * d + q, at(-d, q), y, up).start()
+
+        @pl.when((z > 0) & (z + d <= 3))
+        def _():
+            half_copy(T_ZDOWN + 2 * d + q, at(d, q), y, down).start()
+
+    def take_z(d, q):
+        @pl.when(z - 1 - d >= 0)
+        def _():
+            half_copy(T_ZUP + 2 * d + q, at(-1 - d, q), y, up).wait_recv()
+            half_copy(T_YUP + 2 * d + q, at(-1 - d, q), y, py).start()
+
+        @pl.when(z + 1 + d <= 3)
+        def _():
+            half_copy(T_ZDOWN + 2 * d + q, at(1 + d, q), y, down).wait_recv()
+            half_copy(T_YDOWN + 2 * d + q, at(1 + d, q), y, py).start()
+
+        if d < 2:
+            send_z(d + 1, q)
+
+    def take_y(d, q):
+        @pl.when(z - 1 - d >= 0)
+        def _():
+            half_copy(T_YUP + 2 * d + q, at(-1 - d, q), 1 - y, py).wait_recv()
+            w_copy(T_CORE + 2 + 2 * (2 - d) + q, at(-1 - d, q), pc).start()
+
+        @pl.when(z + 1 + d <= 3)
+        def _():
+            half_copy(T_YDOWN + 2 * d + q, at(1 + d, q), 1 - y, py).wait_recv()
+            w_copy(T_CORE + 2 + 2 * d + q, at(1 + d, q), pc).start()
+
     tok_copy = remote(T_TOK, block(tok_ref, 1 - x, half), xs.at[x], px)
     cot_copy = remote(T_COT, block(cot_ref, 1 - x, half), gs.at[x], px)
     weights[pl.ds(pl.multiple_of(s * shard, shard), shard), :] = w_ref[...]
     other_x = s + 2 - 4 * x
-    carried = z * 4 + 2 * y + c
-
-    def start_z():
-        for j in (1, 2, 3):
-            w_copy(T_Z + j - 1, carried, pz[j]).start()
-
-    @pl.when(x == y)
-    def _():
-        w_copy(T_SIDE, s, px).start()
-        start_z()
-
+    half_copy(T_SIDE, s, y, px).start()
+    send_z(0, 0)
+    half_copy(T_SIDE + 1, s, 1 - y, px).start()
     tok_copy.start()
     w_copy(T_CORE, s, pc).start()
 
@@ -90,17 +129,9 @@
 
     xs[x] = tok_ref[pl.ds(pl.multiple_of(x * half, half), half), :]
     gs[x] = cot_ref[pl.ds(pl.multiple_of(x * half, half), half), :]
+    half_copy(T_SIDE, other_x, y, px).wait_recv()
+    send_z(0, 1)
     normalize(x)
-
-    @pl.when(x != y)
-    def _():
-        w_copy(T_SIDE, other_x, px).wait_recv()
-        start_z()
-        w_copy(T_SIDE, other_x, py).start()
-
-    tok_copy.wait_recv()
-    normalize(1 - x)
-    cot_copy.start()
 
     @pl.when(z == 0)
     def _():
@@ -112,38 +143,19 @@
         taps[3 * half :, :] = jnp.zeros((half, width), BF16)
         grads[3 * half :, :] = jnp.zeros((half, width), BF16)
 
-    @pl.when(x == y)
-    def _():
-        w_copy(T_SIDE, other_x, py).wait_recv()
-
+    take_z(0, 0)
+    half_copy(T_SIDE + 1, other_x, 1 - y, px).wait_recv()
     w_copy(T_CORE + 1, other_x, pc).start()
-    for j in (1, 3, 2):
-        index = ((z + 4 - j) % 4) * 4 + 2 * y + c
-        w_copy(T_Z + j - 1, index, pz[j]).wait_recv()
-        w_copy(T_Y + j - 1, index, py).start()
-        w_copy(T_CORE + 1 + j, index, pc).start()
-    for j in (1, 3, 2):
-        index = ((z + 4 - j) % 4) * 4 + 2 * (1 - y) + c
-        w_copy(T_Y + j - 1, index, py).wait_recv()
-        w_copy(T_CORE + 4 + j, index, pc).start()
-    across = 1 - c
-    own_core = [z * 4 + 2 * x, z * 4 + 2 * (1 - x)]
-    own_core += [((z + 4 - j) % 4) * 4 + 2 * y for j in (1, 2, 3)]
-    own_core += [((z + 4 - j) % 4) * 4 + 2 * (1 - y) for j in (1, 2, 3)]
-    for q, index in enumerate(own_core):
-        w_copy(T_CORE + q, index + across, pc).wait_recv()
-
-    @pl.when(z > 0)
-    def _():
-        up_copy.wait_recv()
-
-    @pl.when(z < 3)
-    def _():
-        down_copy.wait_recv()
-
-    cot_copy.wait_recv()
-
-    part = width // 3
+    take_z(0, 1)
+    tok_copy.wait_recv()
+    cot_copy.start()
+    normalize(1 - x)
+    take_z(1, 0)
+    take_y(0, 0)
+    take_z(1, 1)
+    take_y(0, 1)
+
+    part = width // 2
     root = math.sqrt(2.0 / math.pi)
 
     def pup(n):
@@ -158,8 +170,12 @@
             T_PDOWN + n, grads.at[pl.ds(half, half), cols], grads.at[pl.ds(3 * half, half), cols], down
         )
 
-    @pl.loop(0, 3)
-    def _(n):
+    def out_copy(n):
+        cols = pl.ds(pl.multiple_of(n * part, part), part)
+        there = out_ref.at[pl.ds(pl.multiple_of(x * half, half), half), cols]
+        return remote(T_OUT + n, outs.at[1 - x, :, cols], there, px)
+
+    def forward(n):
         cols = pl.ds(pl.multiple_of(n * part, part), part)
         pre = jnp.zeros((rows, part), F32)
         for k in range(3):
@@ -176,6 +192,7 @@
         value = xs[:, :, cols].reshape(rows, part).astype(F32)
         grad = gs[:, :, cols].reshape(rows, part).astype(F32)
         outs[:, :, cols] = (value + pre * cdf).astype(BF16).reshape(2, half, part)
+        out_copy(n).start()
         d_pre = grad * slope
         grads[half : 3 * half, cols] = d_pre.astype(BF16)
 
@@ -189,8 +206,56 @@
 
         gt[cols, :] = d_pre.T.astype(BF16)
 
-    out_copy = remote(T_OUT, outs.at[1 - x], block(out_ref, x, half), px)
-    out_copy.start()
+    def core_arrival(q, index):
+        w_copy(T_CORE + q, index + 1 - 2 * c, pc).wait_recv()
+
+    def layer_arrival(d):
+        for q in (0, 1):
+            core_arrival(2 + 2 * (d - 1) + q, ((z + d) % 4) * 4 + (2 * x if q == 0 else 2 * (1 - x)) + c)
+
+    near = z // 2
+
+    @pl.when(z > 0)
+    def _():
+        up_copy.wait_recv()
+
+    @pl.when(z < 3)
+    def _():
+        down_copy.wait_recv()
+
+    cot_copy.wait_recv()
+    core_arrival(0, s)
+    core_arrival(1, other_x)
+
+    @pl.when(z % 2 == 0)
+    def _():
+        layer_arrival(1)
+
+    @pl.when(z % 2 == 1)
+    def _():
+        layer_arrival(3)
+
+    @pl.loop(0, 2)
+    def _(turn):
+        @pl.when(turn == 1)
+        def _():
+            for q in (0, 1):
+                take_z(2, q)
+                take_y(1, q)
+            for q in (0, 1):
+                take_y(2, q)
+            layer_arrival(2)
+
+            @pl.when(z % 2 == 0)
+            def _():
+                layer_arrival(3)
+
+            @pl.when(z % 2 == 1)
+            def _():
+                layer_arrival(1)
+
+        forward(near + turn - 2 * near * turn)
+
     for source in range(16):
         place = (source % 2) * 8 + ((source // 2) % 2) * 4 + source // 4
         gtp[place * shard : (place + 1) * shard, :] = gt[source * shard : (source + 1) * shard, :]
@@ -261,12 +326,12 @@
 
     @pl.when(z > 0)
     def _():
-        for n in range(3):
+        for n in range(2):
             pup(n).wait_recv()
 
     @pl.when(z < 3)
     def _():
-        for n in range(3):
+        for n in range(2):
             pdown(n).wait_recv()
 
     input_gradient(1 - x)
@@ -280,26 +345,47 @@
     over_z(1)
     over_z(2)
 
-    out_copy.wait_recv()
+    for n in range(2):
+        out_copy(n).wait_recv()
+        out_copy(n).wait_send()
     dtok_copy.wait_recv()
 
-    for copy in (tok_copy, cot_copy, out_copy, dtok_copy):
+    for copy in (tok_copy, cot_copy, dtok_copy):
         copy.wait_send()
 
     @pl.when(z > 0)
     def _():
         down_copy.wait_send()
-        for n in range(3):
+        for n in range(2):
             pdown(n).wait_send()
 
     @pl.when(z < 3)
     def _():
         up_copy.wait_send()
-        for n in range(3):
+        for n in range(2):
             pup(n).wait_send()
 
-    for t in [T_SIDE] + [T_Z + j for j in range(3)] + [T_Y + j for j in range(3)]:
-        w_copy(t, s, px).wait_send()
+    for t in (T_SIDE, T_SIDE + 1):
+        half_copy(t, s, y, px).wait_send()
+    for d in range(3):
+        for q in (0, 1):
+
+            @pl.when((z < 3) & (z - d >= 0))
+            def _():
+                half_copy(T_ZUP + 2 * d + q, s, y, up).wait_send()
+
+            @pl.when((z > 0) & (z + d <= 3))
+            def _():
+                half_copy(T_ZDOWN + 2 * d + q, s, y, down).wait_send()
+
+            @pl.when(z - 1 - d >= 0)
+            def _():
+                half_copy(T_YUP + 2 * d + q, s, y, py).wait_send()
+
+            @pl.when(z + 1 + d <= 3)
+            def _():
+                half_copy(T_YDOWN + 2 * d + q, s, y, py).wait_send()
+
     for q in range(8):
         w_copy(T_CORE + q, s, pc).wait_send()
     for k in range(3):

time: 91.6 us -> 83.6 us (0.913)
  the two profiles are of different devices: /device:TPU:11 before, /device:TPU:0 now
where the time goes in v2:
time: 83.6 us; the launch traced here: 83.4 us
  Pallas kernels  78.7 us (94%)
  local copies, waits for them, and re-layouts  4.04 us (5%)
    pallas_call x1, Pallas kernels, fused(): pl.pallas_call(functools.partial(kernel, scale), out_shape=(jax.ShapeDtyp...  78.7 us
    unnamed x4, local copies, waits for them, and re-layouts  2.29 us

profile of v2, /device:TPU:0, one launch (start us, length us, event | category | flops | bytes accessed | tf_op | source)
XLA Modules:
  0.0 83.4 jit_solution(16581517263943932255)
XLA Ops:
  0.6 1.0 %copy.11 = bf16[3,6,8,768]{3,2,0,1:T(8,128)(2,1)S(1)} copy(bf16[3,6,8,768]{3,2,1,0:T(8,128)(2,1)} %bitcast.9) | data formatting | bytes 442368 | tf_op jit(solution)/shard_map/reshape | solution.py:440
  1.6 78.7 %shard_map.58 = (bf16[512,768]{1,0:T(8,128)(2,1)S(1)}, bf16[512,768]{1,0:T(8,128)(2,1)}, f32[48,2304]{1,0:T(8,128)S(1)}) custom-call(bf16[512,768]{1,0:T(8,128)(2,1)} %tok_ref.1, bf16[48,2304]{1,0:T(8,128)(2,1)S(1)} %bitcast.7, bf16[512,768]{1,0:T(8,128)(2,1)} %cot_ref.1), custom_call_target="tpu_custom_call" | custom-call | flops 5435817984 | bytes 4718592 | tf_op jit(solution)/shard_map/pallas_call | solution.py:404
  80.3 0.8 copy.13
  81.1 0.0 copy-start
  81.1 0.9 %copy.16 = bf16[512,768]{1,0:T(8,128)(2,1)} copy(bf16[512,768]{1,0:T(8,128)(2,1)S(1)} %get-tuple-element.18) | data formatting | bytes 1572864
  82.0 0.5 copy-done
  82.5 0.9 %copy.17 = bf16[512,768]{1,0:T(8,128)(2,1)} copy(bf16[512,768]{1,0:T(8,128)(2,1)S(1)} %copy-done) | data formatting | bytes 1572864
Async XLA Ops:
  81.1 1.4 %copy-start = (bf16[512,768]{1,0:T(8,128)(2,1)S(1)}, bf16[512,768]{1,0:T(8,128)(2,1)}, u32[]{:S(2)}) copy-start(bf16[512,768]{1,0:T(8,128)(2,1)} %get-tuple-element.19) | copy-start | bytes 2359300

commit v3 on v2

--- a/solution.py
+++ b/solution.py
@@ -15,12 +15,12 @@
 
 T_TOK, T_COT, T_UP, T_DOWN, T_SIDE, T_CORE = 0, 1, 2, 3, 4, 6
 T_ZUP, T_ZDOWN, T_YUP, T_YDOWN = 14, 20, 26, 32
-T_OUT, T_DTOK, T_PUP, T_PDOWN, T_RC, T_RX, T_RZ, T_COUNT = 38, 40, 41, 43, 45, 48, 51, 60
+T_OUT, T_DTOK, T_PUP, T_PDOWN, T_RC, T_RX, T_RZ, T_COUNT = 38, 40, 41, 43, 45, 51, 57, 66
 
 
 def kernel(
     scale, tok_ref, w_ref, cot_ref, out_ref, dtok_ref, dw_ref,
-    xs, gs, taps, grads, weights, gt, gtp, sums, core_send, core_recv,
+    xs, gs, taps, grads, weights, gtp, sums, core_send, core_recv,
     x_send, x_recv, z_sum, z_send, z_recv, outs, dtoks, send_sem, recv_sem,
 ):
     rows, width = tok_ref.shape
@@ -204,7 +204,12 @@
         def _():
             pdown(n).start()
 
-        gt[cols, :] = d_pre.T.astype(BF16)
+        turned = d_pre.T.astype(BF16)
+        for source in range(8):
+            place = n * 8 + (source % 2) * 4 + ((source // 2) % 2) * 2 + source // 4
+            gtp[pl.ds(pl.multiple_of(place * shard, shard), shard), :] = turned[
+                source * shard : (source + 1) * shard
+            ]
 
     def core_arrival(q, index):
         w_copy(T_CORE + q, index + 1 - 2 * c, pc).wait_recv()
@@ -215,91 +220,59 @@
 
     near = z // 2
 
-    @pl.when(z > 0)
-    def _():
-        up_copy.wait_recv()
-
-    @pl.when(z < 3)
-    def _():
-        down_copy.wait_recv()
-
-    cot_copy.wait_recv()
-    core_arrival(0, s)
-    core_arrival(1, other_x)
-
-    @pl.when(z % 2 == 0)
-    def _():
-        layer_arrival(1)
-
-    @pl.when(z % 2 == 1)
-    def _():
-        layer_arrival(3)
-
-    @pl.loop(0, 2)
-    def _(turn):
-        @pl.when(turn == 1)
-        def _():
-            for q in (0, 1):
-                take_z(2, q)
-                take_y(1, q)
-            for q in (0, 1):
-                take_y(2, q)
-            layer_arrival(2)
-
-            @pl.when(z % 2 == 0)
-            def _():
-                layer_arrival(3)
-
-            @pl.when(z % 2 == 1)
-            def _():
-                layer_arrival(1)
-
-        forward(near + turn - 2 * near * turn)
-
-    for source in range(16):
-        place = (source % 2) * 8 + ((source // 2) % 2) * 4 + source // 4
-        gtp[place * shard : (place + 1) * shard, :] = gt[source * shard : (source + 1) * shard, :]
-    out_ref[pl.ds(pl.multiple_of(x * half, half), half), :] = outs[x]
-
-    most = 8 * shard
-
-    def core_copy(k):
-        return remote(T_RC + k, core_send.at[k], core_recv.at[k], pc)
-
-    def x_copy(k):
-        return remote(T_RX + k, x_send.at[k], x_recv.at[k], px)
-
-    def z_copy(k, j):
-        there = block(z_send.at[k], (z + j) % 4, shard)
-        return remote(T_RZ + 3 * k + j - 1, there, z_recv.at[k, j - 1], pz[j])
-
-    def weight_term(k):
+    most = 4 * shard
+
+    def core_copy(u):
+        return remote(T_RC + u, core_send.at[u], core_recv.at[u], pc)
+
+    def x_copy(u):
+        return remote(T_RX + u, x_send.at[u], x_recv.at[u], px)
+
+    def z_copy(u, layer):
+        j = (layer - z + 4) % 4
+        k = u % 3
+        there = block(z_send.at[u], layer % 2, shard)
+        return remote(
+            T_RZ + 3 * k + j - 1, there, z_recv.at[k, j - 1], (y, layer * 4 + 2 * x + c)
+        )
+
+    def z_targets(u):
+        if u < 3:
+            return [near * 2 + 1 - z % 2]
+        return [(1 - near) * 2, (1 - near) * 2 + 1]
+
+    def weight_term(u):
+        k = u % 3
+        n = near if u < 3 else 1 - near
         right = taps[k * half : k * half + rows, :]
-        there = gtp[pl.ds(pl.multiple_of((1 - c) * most, most), most), :]
-        core_send[k] = jnp.dot(there, right, preferred_element_type=F32).astype(BF16)
-        core_copy(k).start()
-        here = gtp[pl.ds(pl.multiple_of(c * most, most), most), :]
-        sums[k] = jnp.dot(here, right, preferred_element_type=F32)
-
-    def over_core(k):
-        core_copy(k).wait_recv()
-        there = pl.ds(pl.multiple_of((1 - x) * 4 * shard, 4 * shard), 4 * shard)
-        x_send[k] = (sums[k, there, :] + core_recv[k, there, :].astype(F32)).astype(BF16)
-        x_copy(k).start()
-
-    def over_x(k):
-        x_copy(k).wait_recv()
-        here = pl.ds(pl.multiple_of(x * 4 * shard, 4 * shard), 4 * shard)
-        total = sums[k, here, :] + core_recv[k, here, :].astype(F32) + x_recv[k].astype(F32)
-        z_sum[k] = total
-        z_send[k] = total.astype(BF16)
+        there = gtp[pl.ds(pl.multiple_of((2 * n + 1 - c) * most, most), most), :]
+        core_send[u] = jnp.dot(there, right, preferred_element_type=F32).astype(BF16)
+        core_copy(u).start()
+        here = gtp[pl.ds(pl.multiple_of((2 * n + c) * most, most), most), :]
+        sums[u] = jnp.dot(here, right, preferred_element_type=F32)
+
+    def over_core(u):
+        core_copy(u).wait_recv()
+        there = pl.ds(pl.multiple_of((1 - x) * 2 * shard, 2 * shard), 2 * shard)
+        x_send[u] = (sums[u, there, :] + core_recv[u, there, :].astype(F32)).astype(BF16)
+        x_copy(u).start()
+
+    def over_x(u):
+        x_copy(u).wait_recv()
+        here = pl.ds(pl.multiple_of(x * 2 * shard, 2 * shard), 2 * shard)
+        total = sums[u, here, :] + core_recv[u, here, :].astype(F32) + x_recv[u].astype(F32)
+        if u < 3:
+            z_sum[u] = total
+        z_send[u] = total.astype(BF16)
+        for layer in z_targets(u):
+            z_copy(u, layer).start()
+
+    def over_z(k):
+        total = z_sum[k, pl.ds(pl.multiple_of((z % 2) * shard, shard), shard), :]
         for j in (1, 2, 3):
-            z_copy(k, j).start()
-
-    def over_z(k):
-        total = z_sum[k, pl.ds(pl.multiple_of(z * shard, shard), shard), :]
-        for j in (1, 2, 3):
-            z_copy(k, j).wait_recv()
+            remote(
+                T_RZ + 3 * k + j - 1, block(z_send.at[k], 0, shard), z_recv.at[k, j - 1], pz[j]
+            ).wait_recv()
             total = total + z_recv[k, j - 1].astype(F32)
         dw_ref[:, k * width : (k + 1) * width] = total * scale
 
@@ -317,12 +290,60 @@
         dtoks[slot] = (grad + inv * total - value * inv * inv * inv * inner).astype(BF16)
 
     dtok_copy = remote(T_DTOK, dtoks.at[1 - x], block(dtok_ref, x, half), px)
+
+    @pl.when(z > 0)
+    def _():
+        up_copy.wait_recv()
+
+    @pl.when(z < 3)
+    def _():
+        down_copy.wait_recv()
+
+    cot_copy.wait_recv()
+    core_arrival(0, s)
+    core_arrival(1, other_x)
+
+    @pl.when(z % 2 == 0)
+    def _():
+        layer_arrival(1)
+
+    @pl.when(z % 2 == 1)
+    def _():
+        layer_arrival(3)
+
+    forward(near)
     weight_term(0)
+    for q in (0, 1):
+        take_z(2, q)
+        take_y(1, q)
     weight_term(1)
     over_core(0)
+    for q in (0, 1):
+        take_y(2, q)
     weight_term(2)
     over_core(1)
     over_core(2)
+    layer_arrival(2)
+
+    @pl.when(z % 2 == 0)
+    def _():
+        layer_arrival(3)
+
+    @pl.when(z % 2 == 1)
+    def _():
+        layer_arrival(1)
+
+    forward(1 - near)
+    weight_term(3)
+    over_x(0)
+    weight_term(4)
+    over_core(3)
+    over_x(1)
+    weight_term(5)
+    over_core(4)
+    over_x(2)
+    over_core(5)
+    out_ref[pl.ds(pl.multiple_of(x * half, half), half), :] = outs[x]
 
     @pl.when(z > 0)
     def _():
@@ -336,11 +357,11 @@
 
     input_gradient(1 - x)
     dtok_copy.start()
-    over_x(0)
+    over_x(3)
     input_gradient(x)
     dtok_ref[pl.ds(pl.multiple_of(x * half, half), half), :] = dtoks[x]
-    over_x(1)
-    over_x(2)
+    over_x(4)
+    over_x(5)
     over_z(0)
     over_z(1)
     over_z(2)
@@ -388,11 +409,11 @@
 
     for q in range(8):
         w_copy(T_CORE + q, s, pc).wait_send()
-    for k in range(3):
-        core_copy(k).wait_send()
-        x_copy(k).wait_send()
-        for j in (1, 2, 3):
-            z_copy(k, j).wait_send()
+    for u in range(6):
+        core_copy(u).wait_send()
+        x_copy(u).wait_send()
+        for layer in z_targets(u):
+            z_copy(u, layer).wait_send()
 
 
 def fused(tokens, weight, cotangent):
@@ -417,14 +438,13 @@
             pltpu.VMEM((4 * half, width), BF16),
             pltpu.VMEM((width, 3 * width), BF16),
             pltpu.VMEM((width, rows), BF16),
-            pltpu.VMEM((width, rows), BF16),
-            pltpu.VMEM((3, 8 * shard, width), F32),
-            pltpu.VMEM((3, 8 * shard, width), BF16),
-            pltpu.VMEM((3, 8 * shard, width), BF16),
-            pltpu.VMEM((3, 4 * shard, width), BF16),
-            pltpu.VMEM((3, 4 * shard, width), BF16),
-            pltpu.VMEM((3, 4 * shard, width), F32),
-            pltpu.VMEM((3, 4 * shard, width), BF16),
+            pltpu.VMEM((6, 4 * shard, width), F32),
+            pltpu.VMEM((6, 4 * shard, width), BF16),
+            pltpu.VMEM((6, 4 * shard, width), BF16),
+            pltpu.VMEM((6, 2 * shard, width), BF16),
+            pltpu.VMEM((6, 2 * shard, width), BF16),
+            pltpu.VMEM((3, 2 * shard, width), F32),
+            pltpu.VMEM((6, 2 * shard, width), BF16),
             pltpu.VMEM((3, 3, shard, width), BF16),
             pltpu.VMEM((2, half, width), BF16),
             pltpu.VMEM((2, half, width), BF16),

time: 83.6 us -> 81 us (0.969)
  Pallas kernels: 78.7 us -> 76.1 us
    pallas_call x1, Pallas kernels: 78.7 us -> 76.1 us  [fused(): pl.pallas_call(functools.partial(kernel, scale), out_shape=(jax.ShapeDtyp...]
where the time goes in v3:
time: 81 us; the launch traced here: 80.8 us
  Pallas kernels  76.1 us (94%)
  local copies, waits for them, and re-layouts  4.04 us (5%)
    pallas_call x1, Pallas kernels, fused(): pl.pallas_call(functools.partial(kernel, scale), out_shape=(jax.ShapeDtyp...  76.1 us
    unnamed x4, local copies, waits for them, and re-layouts  2.29 us

profile of v3, /device:TPU:0, one launch (start us, length us, event | category | flops | bytes accessed | tf_op | source)
XLA Modules:
  0.0 80.8 jit_solution(4250909892932685649)
XLA Ops:
  0.6 1.0 %copy.11 = bf16[3,6,8,768]{3,2,0,1:T(8,128)(2,1)S(1)} copy(bf16[3,6,8,768]{3,2,1,0:T(8,128)(2,1)} %bitcast.9) | data formatting | bytes 442368 | tf_op jit(solution)/shard_map/reshape | solution.py:460
  1.6 76.1 %shard_map.58 = (bf16[512,768]{1,0:T(8,128)(2,1)S(1)}, bf16[512,768]{1,0:T(8,128)(2,1)}, f32[48,2304]{1,0:T(8,128)S(1)}) custom-call(bf16[512,768]{1,0:T(8,128)(2,1)} %tok_ref.1, bf16[48,2304]{1,0:T(8,128)(2,1)S(1)} %bitcast.7, bf16[512,768]{1,0:T(8,128)(2,1)} %cot_ref.1), custom_call_target="tpu_custom_call" | custom-call | flops 5435817984 | bytes 4718592 | tf_op jit(solution)/shard_map/pallas_call | solution.py:425
  77.7 0.8 copy.13
  78.5 0.0 copy-start
  78.5 0.9 %copy.16 = bf16[512,768]{1,0:T(8,128)(2,1)} copy(bf16[512,768]{1,0:T(8,128)(2,1)S(1)} %get-tuple-element.18) | data formatting | bytes 1572864
  79.4 0.5 copy-done
  79.9 0.9 %copy.17 = bf16[512,768]{1,0:T(8,128)(2,1)} copy(bf16[512,768]{1,0:T(8,128)(2,1)S(1)} %copy-done) | data formatting | bytes 1572864
Async XLA Ops:
  78.5 1.4 %copy-start = (bf16[512,768]{1,0:T(8,128)(2,1)S(1)}, bf16[512,768]{1,0:T(8,128)(2,1)}, u32[]{:S(2)}) copy-start(bf16[512,768]{1,0:T(8,128)(2,1)} %get-tuple-element.19) | copy-start | bytes 2359300
